TPU v7x, 32 devices: a whole 2x2x4 slice. The times are simulated.
32 devices in a mesh: dp: 4 (over x, core), heads: 8 (over z, y).
Axes of the slice: x: 2, y: 2, z: 4, core: 2. Of those that a mesh axis runs over, the one named last changes fastest.
Arguments:
- hidden: bfloat16 [4096, 2048], P(('dp', 'heads')), may hold values from -6 to 6
- seq_lens: int32 [4, 3], P('dp'), may hold values from 1 to 1021, as said below
- norm_w: bfloat16 [2048], P(('dp', 'heads')), may hold values from 0.5 to 1.5
- w_in: bfloat16 [2048, 8512], P(('dp', 'heads')), may hold values from -0.125 to 0.125
- conv_w: bfloat16 [4, 4352], P(None, ('dp', 'heads')), may hold values from -3 to 3
- conv_b: bfloat16 [4352], P(('dp', 'heads')), may hold values from -2 to 2
- dt_bias: float32 [64], P('heads'), may hold values from -6.9 to -2.3
- a_log: float32 [64], P('heads'), may hold values from -2 to 1
- skip_gain: float32 [64], P('heads'), may hold values from 0.5 to 1.5
- gate_w: bfloat16 [4096], P(('dp', 'heads')), may hold values from 0.5 to 1.5
- w_out: bfloat16 [4096, 2048], P(('dp', 'heads')), may hold values from -0.09375 to 0.09375
- cotangent: bfloat16 [4096, 2048], P(('dp', 'heads')), may hold values from -6 to 6
Outputs:
- output: bfloat16 [4096, 2048], P(('dp', 'heads'))
- input_grad: float32 [4096, 2048], P(('dp', 'heads'))
- norm_w_grad: float32 [2048], P(('dp', 'heads'))
- w_in_grad: float32 [2048, 8512], P(('dp', 'heads'))
- conv_w_grad: float32 [4, 4352], P(None, ('dp', 'heads'))
- conv_b_grad: float32 [4352], P(('dp', 'heads'))
- dt_bias_grad: float32 [64], P('heads')
- a_log_grad: float32 [64], P('heads')
- skip_gain_grad: float32 [64], P('heads')
- gate_w_grad: float32 [4096], P(('dp', 'heads'))
- w_out_grad: float32 [4096, 2048], P(('dp', 'heads'))
Inputs may be any that keep to these rules, and one draw needn't show every extreme that they name: `seq_lens`: row g holds the lengths of the 3 sequences that lie one after another from the first token of data group g; padding fills the rest of the group's 1024 tokens and is at least one token.
All inputs are finite; a program needn't handle non-finite values.
Results may differ from a plain program's by a relative error of at most 0.012.
Values may be sent and summed in bfloat16 or wider, within the bound.
No kernel may reach another device: no remote copies, remote signals or barrier semaphores. Data moves between devices by JAX's collectives and lax.ppermute only.
A program may use at most 448 MiB of HBM per device.

v0:
```python
import jax
import jax.numpy as jnp
from jax import lax
from jax.sharding import PartitionSpec as P

P_SIZE = 64
N = 128
CONV_K = 4
BLOCK_LEN = 256
SEQS = 3
DI = 4096
CONV_CH = 4352


EPS = 1e-05


def from_behind(block, axis, distance):
    devices = range(lax.axis_size(axis))
    route = [(i - distance, i) for i in devices if i - distance in devices]
    return lax.ppermute(block, axis, route)


def shortened(array):

    def short(part):
        return part.astype(jnp.bfloat16) if part.dtype == jnp.float32 else part

    return jax.tree.map(short, array)


def rms_norm(values, gain_row):
    return values * lax.rsqrt(jnp.mean(values * values, axis=-1, keepdims=True) + EPS) * gain_row


def segment_of(positions, seq_ends):
    counted = jnp.sum((positions[:, None] >= seq_ends[None, :]).astype(jnp.int32), axis=1)
    return jnp.where(positions < 0, -1, counted)


def conv_apply(extended, seg_ext, conv_taps, conv_bias):
    row_count = extended.shape[0] - (CONV_K - 1)
    own_seg = seg_ext[CONV_K - 1 :]
    total = jnp.zeros((row_count, extended.shape[1]), extended.dtype) + conv_bias[None, :]
    for tap_index in range(CONV_K):
        same_seg = (seg_ext[tap_index : tap_index + row_count] == own_seg)[:, None]
        total = total + jnp.where(
            same_seg,
            conv_taps[tap_index][None, :] * extended[tap_index : tap_index + row_count],
            0.0,
        )
    return jax.nn.silu(total)


def ssd_scan(x_heads, dt_heads, a_neg, b_state, c_state, seg_group, skip_part):
    highest = lax.Precision.HIGHEST
    length, head_count, head_width = x_heads.shape
    blocks = length // BLOCK_LEN
    x_block = x_heads.reshape(blocks, BLOCK_LEN, head_count, head_width)
    dt_block = dt_heads.reshape(blocks, BLOCK_LEN, head_count)
    cum_decay = jnp.cumsum(dt_block * a_neg[None, None, :], axis=1)
    b_block = b_state.reshape(blocks, BLOCK_LEN, b_state.shape[1])
    c_block = c_state.reshape(blocks, BLOCK_LEN, c_state.shape[1])
    seg_block = seg_group.reshape(blocks, BLOCK_LEN)
    positions_in = jnp.arange(BLOCK_LEN, dtype=jnp.int32)
    linked = (seg_block[:, :, None] == seg_block[:, None, :]) & (
        positions_in[:, None] >= positions_in[None, :]
    )[None]
    linked = linked[..., None]
    log_gaps = cum_decay[:, :, None, :] - cum_decay[:, None, :, :]
    decays = jnp.where(linked, jnp.exp(jnp.where(linked, log_gaps, 0.0)), 0.0)
    scores = jnp.einsum("cqn,csn->cqs", c_block, b_block, precision=highest)
    mixing = scores[..., None] * decays * dt_block[:, None, :, :]
    inner_part = jnp.einsum("cqsh,cshp->cqhp", mixing, x_block, precision=highest)
    last_seg = seg_block[:, -1:]
    tail_weight = (
        jnp.where(
            (seg_block == last_seg)[..., None], jnp.exp(cum_decay[:, -1:, :] - cum_decay), 0.0
        )
        * dt_block
    )
    states = jnp.einsum("csn,csh,cshp->chpn", b_block, tail_weight, x_block, precision=highest)
    prev_end = jnp.concatenate([jnp.full((1,), -1, jnp.int32), seg_block[:-1, -1]])
    carry_keep = jnp.where(
        (seg_block[:, -1] == prev_end)[:, None], jnp.exp(cum_decay[:, -1, :]), 0.0
    )

    def advance(carried, inputs):
        block_state, block_keep = inputs
        return (block_state + block_keep[:, None, None] * carried, carried)

    start_state = jnp.zeros(states.shape[1:], states.dtype)
    _, entering = lax.scan(advance, start_state, (states, carry_keep))
    enter_weight = jnp.where((seg_block == prev_end[:, None])[..., None], jnp.exp(cum_decay), 0.0)
    outer_part = (
        jnp.einsum("cqn,chpn->cqhp", c_block, entering, precision=highest) * enter_weight[..., None]
    )
    result = inner_part + outer_part + skip_part[None, None, :, None] * x_block
    return result.reshape(length, head_count, head_width)


def shards(
    hidden,
    seq_lens,
    norm_w,
    w_in,
    conv_w,
    conv_b,
    dt_bias,
    a_log,
    skip_gain,
    gate_w,
    w_out,
    cotangent,
):
    rows_dev = hidden.shape[0]
    width_axis = lax.axis_size("heads")
    head_index = lax.axis_index("heads")
    group_len = rows_dev * width_axis
    gathered = (
        lax.all_gather(norm_w, ("dp", "heads"), axis=0, tiled=True),
        lax.all_gather(w_in, ("dp", "heads"), axis=0, tiled=True),
        lax.all_gather(conv_w, ("dp", "heads"), axis=1, tiled=True),
        lax.all_gather(conv_b, ("dp", "heads"), axis=0, tiled=True),
        lax.all_gather(gate_w, ("dp", "heads"), axis=0, tiled=True),
        lax.all_gather(w_out, ("dp", "heads"), axis=0, tiled=True),
    )
    norm_full, w_in_full, conv_full, bias_full, gate_full, w_out_full = gathered
    seq_ends = jnp.cumsum(seq_lens[0])
    seg_group = segment_of(jnp.arange(group_len, dtype=jnp.int32), seq_ends)
    first_row = head_index * rows_dev
    seg_ext = segment_of(
        first_row - (CONV_K - 1) + jnp.arange(rows_dev + CONV_K - 1, dtype=jnp.int32), seq_ends
    )
    seg_own = seg_ext[CONV_K - 1 :]
    residual = hidden.astype(jnp.float32)
    normed, norm_pull = jax.vjp(rms_norm, residual, norm_full.astype(jnp.float32))
    normed_low = normed.astype(jnp.bfloat16)
    projected = jnp.dot(normed_low, w_in_full, preferred_element_type=jnp.float32)
    gate_part = projected[:, :DI]
    conv_in = projected[:, DI : DI + CONV_CH]
    dt_low = projected[:, DI + CONV_CH :].astype(jnp.bfloat16)
    rim_rows = from_behind(
        conv_in[rows_dev - (CONV_K - 1) :].astype(jnp.bfloat16), "heads", 1
    ).astype(jnp.float32)
    extended = jnp.concatenate([rim_rows, conv_in], axis=0)

    def conv_local(ext_rows, taps_in, biases_in):
        return conv_apply(ext_rows, seg_ext, taps_in, biases_in)

    conv_out, conv_pull = jax.vjp(
        conv_local, extended, conv_full.astype(jnp.float32), bias_full.astype(jnp.float32)
    )
    x_low = conv_out[:, :DI].astype(jnp.bfloat16)
    b_low = conv_out[:, DI : DI + N].astype(jnp.bfloat16)
    c_low = conv_out[:, DI + N :].astype(jnp.bfloat16)
    x_heads, dt_heads = (
        lax.all_to_all(x_low, "heads", split_axis=1, concat_axis=0, tiled=True),
        lax.all_to_all(dt_low, "heads", split_axis=1, concat_axis=0, tiled=True),
    )
    b_all, c_all = (
        lax.all_gather(b_low, "heads", axis=0, tiled=True),
        lax.all_gather(c_low, "heads", axis=0, tiled=True),
    )
    head_count = dt_heads.shape[1]

    def scan_local(x_in, dt_in, b_in, c_in, bias_in, log_in, skip_in):
        steps_dt = jax.nn.softplus(dt_in + bias_in[None, :])
        mixed_heads = ssd_scan(
            x_in.reshape(group_len, head_count, P_SIZE),
            steps_dt,
            -jnp.exp(log_in),
            b_in,
            c_in,
            seg_group,
            skip_in,
        )
        return mixed_heads.reshape(group_len, head_count * P_SIZE)

    scanned, scan_pull = jax.vjp(
        jax.checkpoint(scan_local),
        x_heads.astype(jnp.float32),
        dt_heads.astype(jnp.float32),
        b_all.astype(jnp.float32),
        c_all.astype(jnp.float32),
        dt_bias,
        a_log,
        skip_gain,
    )
    back_rows = lax.all_to_all(
        scanned.astype(jnp.bfloat16), "heads", split_axis=0, concat_axis=1, tiled=True
    )

    def gate_local(scan_in, gate_in, gain_in):
        return rms_norm(scan_in * jax.nn.silu(gate_in), gain_in)

    gated, gate_pull = jax.vjp(
        gate_local, back_rows.astype(jnp.float32), gate_part, gate_full.astype(jnp.float32)
    )
    gated_low = gated.astype(jnp.bfloat16)
    branch = jnp.dot(gated_low, w_out_full, preferred_element_type=jnp.float32)
    live_rows = (seg_own < SEQS)[:, None]
    output = (residual + jnp.where(live_rows, branch, 0.0)).astype(jnp.bfloat16)
    w_in_back, w_out_back = (w_in_full, w_out_full)
    contract_last = (((1,), (1,)), ((), ()))
    contract_first = (((0,), (0,)), ((), ()))
    grad_branch = jnp.where(live_rows, cotangent, jnp.zeros_like(cotangent))
    grad_gated = lax.dot_general(
        grad_branch, w_out_back, contract_last, preferred_element_type=jnp.float32
    )
    w_out_term = lax.dot_general(
        gated_low, grad_branch, contract_first, preferred_element_type=jnp.float32
    )
    grad_scan_rows, grad_gate_part, grad_gate_gain = gate_pull(grad_gated)
    grad_heads = lax.all_to_all(
        grad_scan_rows.astype(jnp.bfloat16), "heads", split_axis=1, concat_axis=0, tiled=True
    )
    grad_x, grad_dt, grad_b, grad_c, grad_bias, grad_log, grad_skip = scan_pull(
        grad_heads.astype(jnp.float32)
    )
    grad_x_rows, grad_dt_rows = (
        lax.all_to_all(
            grad_x.astype(jnp.bfloat16), "heads", split_axis=0, concat_axis=1, tiled=True
        ),
        lax.all_to_all(
            grad_dt.astype(jnp.bfloat16), "heads", split_axis=0, concat_axis=1, tiled=True
        ),
    )
    grad_b_rows, grad_c_rows = (
        lax.psum_scatter(
            grad_b.astype(jnp.bfloat16), "heads", scatter_dimension=0, tiled=True
        ).astype(jnp.float32),
        lax.psum_scatter(
            grad_c.astype(jnp.bfloat16), "heads", scatter_dimension=0, tiled=True
        ).astype(jnp.float32),
    )
    bias_grad, log_grad, skip_grad = lax.psum((grad_bias, grad_log, grad_skip), "dp")
    grad_conv_out = jnp.concatenate(
        [grad_x_rows.astype(jnp.float32), grad_b_rows, grad_c_rows], axis=1
    )
    grad_ext, grad_taps, grad_biases = conv_pull(grad_conv_out)
    grad_rim = from_behind(shortened(grad_ext[: CONV_K - 1]), "heads", -1)
    grad_conv_in = grad_ext[CONV_K - 1 :] + jnp.concatenate(
        [jnp.zeros((rows_dev - (CONV_K - 1), CONV_CH), jnp.float32), grad_rim], axis=0
    )
    grad_proj = jnp.concatenate(
        [grad_gate_part, grad_conv_in, grad_dt_rows.astype(jnp.float32)], axis=1
    ).astype(jnp.bfloat16)
    grad_normed = lax.dot_general(
        grad_proj, w_in_back, contract_last, preferred_element_type=jnp.float32
    )
    grad_residual, grad_norm_gain = norm_pull(grad_normed)
    input_grad = cotangent.astype(jnp.float32) + grad_residual
    w_in_term = lax.dot_general(
        normed_low, grad_proj, contract_first, preferred_element_type=jnp.float32
    )
    w_in_grad, w_out_grad, norm_grad, gate_grad, taps_grad, biases_grad = (
        lax.psum_scatter(w_in_term, ("dp", "heads"), scatter_dimension=0, tiled=True),
        lax.psum_scatter(w_out_term, ("dp", "heads"), scatter_dimension=0, tiled=True),
        lax.psum_scatter(grad_norm_gain, ("dp", "heads"), scatter_dimension=0, tiled=True),
        lax.psum_scatter(grad_gate_gain, ("dp", "heads"), scatter_dimension=0, tiled=True),
        lax.psum_scatter(grad_taps, ("dp", "heads"), scatter_dimension=1, tiled=True),
        lax.psum_scatter(grad_biases, ("dp", "heads"), scatter_dimension=0, tiled=True),
    )
    return (
        output,
        input_grad,
        norm_grad,
        w_in_grad,
        taps_grad,
        biases_grad,
        bias_grad,
        log_grad,
        skip_grad,
        gate_grad,
        w_out_grad,
    )


def solution(mesh):
    placed = (
        P(("dp", "heads"), None),
        P("dp", None),
        P(("dp", "heads")),
        P(("dp", "heads"), None),
        P(None, ("dp", "heads")),
        P(("dp", "heads")),
        P("heads"),
        P("heads"),
        P("heads"),
        P(("dp", "heads")),
        P(("dp", "heads"), None),
        P(("dp", "heads"), None),
    )
    return jax.shard_map(
        shards,
        mesh=mesh,
        in_specs=placed,
        out_specs=(
            P(("dp", "heads"), None),
            P(("dp", "heads"), None),
            P(("dp", "heads")),
            P(("dp", "heads"), None),
            P(None, ("dp", "heads")),
            P(("dp", "heads")),
            P("heads"),
            P("heads"),
            P("heads"),
            P(("dp", "heads")),
            P(("dp", "heads"), None),
        ),
        check_vma=False,
    )
```

profile of v0, /device:TPU:16, one launch (start us, length us, event | category | flops | bytes accessed | tf_op | source)
XLA Modules:
  0.0 3076.7 jit_solution(9039696529800322366)
XLA Ops:
  11.4 42.5 %all-reduce.19 = (bf16[2048]{0:T(1024)(128)(2,1)S(1)}, bf16[4352]{0:T(1024)(128)(2,1)S(1)}) all-reduce(bf16[2048]{0:T(1024)(128)(2,1)S(1)} %dynamic-update-slice.1, bf16[4352]{0:T(1024)(128)(2,1)S(1)} %dynamic-update-slice), channel_id=1, replica_groups=mesh['dp'=4,'heads'=8] {'dp','heads'}, use_global_device_ids=true, to_apply=%add.12 | all-reduce | flops 6400 | bytes 25600
  53.9 63.8 %all-gather = bf16[32,136,4]{1,2,0:T(4,128)(2,1)S(1)} all-gather(bf16[1,136,4]{1,2,0:T(4,128)(2,1)} %bitcast.267), channel_id=1, replica_groups=mesh['dp'=4,'heads'=8] {'dp','heads'}, dimensions={0}, use_global_device_ids=true | all-gather | bytes 35904 | tf_op jit(solution)/shard_map/all_gather | solution.py:123
  120.7 94.0 %all-gather.5.cloned.1.call-done = bf16[2048,8512]{1,0:T(8,128)(2,1)} async-done(((bf16[64,8512]{1,0:T(8,128)(2,1)}), bf16[2048,8512]{1,0:T(8,128)(2,1)}) %all-gather.5.cloned.1.call-update) | async-done | bytes 34865168 | tf_op jit(solution)/shard_map/all_gather | solution.py:122
  214.7 20.2 fusion.123
  250.6 10.6 multiply_convert_fusion
  261.2 26.2 all_gather.29
  289.6 6.2 all-to-all-start
  295.8 65.8 %all_gather.28 = bf16[1024,128]{0,1:T(8,128)(2,1)S(1)} all-gather(bf16[128,128]{0,1:T(8,128)(2,1)S(1)} %get-tuple-element.398), channel_id=1, replica_groups=mesh['dp'=4,'heads'=8] {'heads'}, dimensions={0}, use_global_device_ids=true | all-gather | bytes 294912 | tf_op jit(solution)/shard_map/all_gather | solution.py:163
  379.3 7.2 fusion.40
  389.0 10.7 all-to-all-start.2
  399.7 67.5 %all-gather.1 = bf16[32,1,128]{2,1,0:T(2,128)(2,1)S(1)} all-gather(bf16[1,1,128]{2,1,0:T(2,128)(2,1)S(1)} %bitcast.270), channel_id=1, replica_groups=mesh['dp'=4,'heads'=8] {'dp','heads'}, dimensions={0}, use_global_device_ids=true | all-gather | bytes 8448 | tf_op jit(solution)/shard_map/all_gather | solution.py:125
  469.6 9.6 multiply_reduce_fusion.6
  484.6 10.6 all-to-all-start.3
  498.5 15.7 all-to-all-done.3
  546.1 9.4 while.50
  562.3 15.2 while.51
  582.0 8.2 fusion.44
  596.6 7.3 all-to-all-start.4
  603.9 16.2 fusion.18
  625.9 4.9 fusion.67
  633.5 53.9 %reduce-scatter.16.cloned.1.call-done = bf16[128,128]{1,0:T(8,128)(2,1)} async-done(((bf16[1024,128]{1,0:T(8,128)(2,1)}), bf16[128,128]{1,0:T(8,128)(2,1)}) %reduce-scatter.16.cloned.1.call-update) | async-done | bytes 32784
  688.2 63.1 %reduce-scatter.14.cloned.1.call-done = bf16[128,128]{1,0:T(8,128)(2,1)} async-done(((bf16[1024,128]{1,0:T(8,128)(2,1)}), bf16[128,128]{1,0:T(8,128)(2,1)}) %reduce-scatter.14.cloned.1.call-update) | async-done | bytes 32784
  752.3 15.2 multiply_reduce_fusion.3
  768.4 17.1 fusion.88
  796.5 10.1 reduce-window.43
  831.8 25.9 fusion.78
  858.9 9.1 fusion.32
  868.8 6.5 all-reduce.18
  875.3 28.0 fusion.71
  903.3 47.7 %all-reduce.17 = (f32[2048]{0:T(1024)S(1)}, f32[4352]{0:T(1024)S(1)}, f32[4096]{0:T(1024)S(1)}) all-reduce(f32[2048]{0:T(1024)S(1)} %get-tuple-element.328, f32[4352]{0:T(1024)S(1)} %copy-done.49, f32[4096]{0:T(1024)S(1)} %copy-done.56), channel_id=4, replica_groups=mesh['dp'=4,'heads'=8] {'dp','heads'}, use_global_device_ids=true, to_apply=%region_29.30.clone | all-reduce | flops 10496 | bytes 83968
  956.7 641.8 %reduce-scatter.12.cloned.1.call-done = f32[128,2048]{1,0:T(8,128)} async-done(((f32[4096,2048]{1,0:T(8,128)}), f32[128,2048]{1,0:T(8,128)}) %reduce-scatter.12.cloned.1.call-update) | async-done | bytes 1048592 | tf_op jit(solution)/shard_map/reduce_scatter | solution.py:259
  1598.6 1470.8 %reduce-scatter.10.cloned.1.call-done = f32[64,8512]{1,0:T(8,128)} async-done(((f32[2048,8512]{1,0:T(8,128)}), f32[64,8512]{1,0:T(8,128)}) %reduce-scatter.10.cloned.1.call-update) | async-done | bytes 2179088 | tf_op jit(solution)/shard_map/reduce_scatter | solution.py:258
  (390 shorter events, 187.5 us)
Async XLA Ops:
  7.2 111.6 %copy-start.9 = (bf16[128,2048]{1,0:T(8,128)(2,1)S(1)}, bf16[128,2048]{1,0:T(8,128)(2,1)}, u32[]{:S(2)}) copy-start(bf16[128,2048]{1,0:T(8,128)(2,1)} %param.18) | copy-start | bytes 1572868
  7.2 112.4 %copy-start.80 = (f32[8]{0:T(128)S(1)}, f32[8]{0:T(128)}, u32[]{:S(2)}) copy-start(f32[8]{0:T(128)} %param.25) | copy-start | bytes 100
  7.2 207.5 %all-gather.5.cloned.1.call-start = ((), (), s32[]{:S(2)}) async-start(), calls=%async_computation.10 | async-start | bytes 36225024 | tf_op jit(solution)/shard_map/all_gather | solution.py:122
  7.9 461.7 %all-gather.7.cloned.1.call-start = ((), (), s32[]{:S(2)}) async-start(), calls=%async_computation.11 | async-start | bytes 17301504 | tf_op jit(solution)/shard_map/all_gather | solution.py:126
  118.8 131.8 %copy-start.39 = (f32[4352]{0:T(1024)}, f32[4352]{0:T(1024)S(1)}, u32[]{:S(2)}) copy-start(f32[4352]{0:T(1024)S(1)} %get-tuple-element.330) | copy-start | bytes 52228
  118.8 131.8 %copy-start.41 = (f32[4352]{0:T(1024)}, f32[4352]{0:T(1024)S(1)}, u32[]{:S(2)}) copy-start(f32[4352]{0:T(1024)S(1)} %get-tuple-element.331) | copy-start | bytes 52228
  118.8 131.8 %copy-start.43 = (f32[4352]{0:T(1024)}, f32[4352]{0:T(1024)S(1)}, u32[]{:S(2)}) copy-start(f32[4352]{0:T(1024)S(1)} %get-tuple-element.332) | copy-start | bytes 52228
  118.8 131.8 %copy-start.45 = (f32[4352]{0:T(1024)}, f32[4352]{0:T(1024)S(1)}, u32[]{:S(2)}) copy-start(f32[4352]{0:T(1024)S(1)} %get-tuple-element.333) | copy-start | bytes 52228
  119.6 115.3 %copy-start.51 = (f32[128]{0:T(128)}, f32[128]{0:T(128)S(1)}, u32[]{:S(2)}) copy-start(f32[128]{0:T(128)S(1)} %fusion.109) | copy-start | bytes 1540
  119.7 130.9 %copy-start.59 = (pred[128]{0:T(512)(128)(4,1)}, pred[128]{0:T(512)(128)(4,1)S(1)}, u32[]{:S(2)}) copy-start(pred[128]{0:T(512)(128)(4,1)S(1)} %get-tuple-element.413) | copy-start | bytes 388
  119.7 130.9 %copy-start.61 = (pred[128]{0:T(512)(128)(4,1)}, pred[128]{0:T(512)(128)(4,1)S(1)}, u32[]{:S(2)}) copy-start(pred[128]{0:T(512)(128)(4,1)S(1)} %get-tuple-element.414) | copy-start | bytes 388
  119.7 130.9 %copy-start.63 = (pred[128]{0:T(512)(128)(4,1)}, pred[128]{0:T(512)(128)(4,1)S(1)}, u32[]{:S(2)}) copy-start(pred[128]{0:T(512)(128)(4,1)S(1)} %get-tuple-element.415) | copy-start | bytes 388
  119.7 349.9 %copy-start.66 = (pred[128]{0:T(512)(128)(4,1)}, pred[128]{0:T(512)(128)(4,1)S(1)}, u32[]{:S(2)}) copy-start(pred[128]{0:T(512)(128)(4,1)S(1)} %get-tuple-element.412) | copy-start | bytes 388
  238.0 10.5 collective-permute-start
  241.9 47.7 %all-to-all-start.1 = ((bf16[128,8,8]{0,2,1:T(8,128)(2,1)}), bf16[128,8,8]{0,2,1:T(8,128)(2,1)S(1)}, u32[]{:S(2)}, u32[]{:S(2)}) async-start(bf16[128,8,8]{0,2,1:T(8,128)(2,1)} %slice_bitcast_fusion), calls=%async_computation.1 | async-start | bytes 32768 | tf_op jit(solution)/shard_map/all_to_all | solution.py:159
  289.6 79.1 %all-to-all-start = ((bf16[128,8,512]{2,0,1:T(8,128)(2,1)}), bf16[128,8,512]{2,0,1:T(8,128)(2,1)S(1)}, u32[]{:S(2)}, u32[]{:S(2)}) async-start(bf16[128,8,512]{2,0,1:T(8,128)(2,1)} %copy.256), calls=%async_computation | async-start | bytes 2097152 | tf_op jit(solution)/shard_map/all_to_all | solution.py:158
  389.0 80.6 %copy-start.32 = (bf16[128,2048]{1,0:T(8,128)(2,1)S(1)}, bf16[128,2048]{1,0:T(8,128)(2,1)}, u32[]{:S(2)}) copy-start(bf16[128,2048]{1,0:T(8,128)(2,1)} %param.29) | copy-start | bytes 1572868
  389.0 78.2 %all-to-all-start.2 = ((bf16[8,128,512]{1,2,0:T(8,128)(2,1)}), bf16[8,128,512]{1,2,0:T(8,128)(2,1)S(1)}, u32[]{:S(2)}, u32[]{:S(2)}) async-start(bf16[8,128,512]{1,2,0:T(8,128)(2,1)} %copy.267), calls=%async_computation.2 | async-start | bytes 2097152 | tf_op jit(solution)/shard_map/all_to_all | solution.py:190
  484.6 29.6 all-to-all-start.3
  596.6 155.6 %all-to-all-start.4 = ((bf16[8,128,512]{1,2,0:T(8,128)(2,1)}), bf16[8,128,512]{1,2,0:T(8,128)(2,1)}, u32[]{:S(2)}, u32[]{:S(2)}) async-start(bf16[8,128,512]{1,2,0:T(8,128)(2,1)} %copy.285), calls=%async_computation.4 | async-start | bytes 2097152 | tf_op jit(solution)/shard_map/all_to_all | solution.py:222
  603.9 83.5 %reduce-scatter.16.cloned.1.call-start = ((), (), s32[]{:S(2)}) async-start(), calls=%async_computation.15 | async-start | bytes 294912
  625.4 125.9 %reduce-scatter.14.cloned.1.call-start = ((), (), s32[]{:S(2)}) async-start(), calls=%async_computation.14 | async-start | bytes 294912
  630.8 121.4 %copy-start.60 = (pred[128]{0:T(512)(128)(4,1)S(1)}, pred[128]{0:T(512)(128)(4,1)}, u32[]{:S(2)}) copy-start(pred[128]{0:T(512)(128)(4,1)} %copy-done.59) | copy-start | bytes 388
  630.8 121.4 %copy-start.62 = (pred[128]{0:T(512)(128)(4,1)S(1)}, pred[128]{0:T(512)(128)(4,1)}, u32[]{:S(2)}) copy-start(pred[128]{0:T(512)(128)(4,1)} %copy-done.61) | copy-start | bytes 388
  630.8 121.4 %copy-start.64 = (pred[128]{0:T(512)(128)(4,1)S(1)}, pred[128]{0:T(512)(128)(4,1)}, u32[]{:S(2)}) copy-start(pred[128]{0:T(512)(128)(4,1)} %copy-done.63) | copy-start | bytes 388
  633.4 322.0 %all-reduce.22.cloned.1.call-start = ((), (), s32[]{:S(2)}) async-start(), calls=%async_computation.16 | async-start | bytes 139264
  768.2 830.3 %reduce-scatter.12.cloned.1.call-start = ((), (), s32[]{:S(2)}) async-start(), calls=%async_computation.13 | async-start | bytes 34603008 | tf_op jit(solution)/shard_map/reduce_scatter | solution.py:259
  817.6 9.3 collective-permute-start.1
  822.6 9.2 all-to-all-start.5
  826.8 2242.5 %reduce-scatter.10.cloned.1.call-start = ((), (), s32[]{:S(2)}) async-start(), calls=%async_computation.12 | async-start | bytes 72450048 | tf_op jit(solution)/shard_map/reduce_scatter | solution.py:258
  875.3 77.5 %copy-start.76 = (f32[128]{0:T(128)S(1)}, f32[128]{0:T(128)}, u32[]{:S(2)}) copy-start(f32[128]{0:T(128)} %copy-done.75) | copy-start | bytes 1540
  875.3 77.5 %copy-start.33 = (bf16[128,2048]{1,0:T(8,128)(2,1)S(1)}, bf16[128,2048]{1,0:T(8,128)(2,1)}, u32[]{:S(2)}) copy-start(bf16[128,2048]{1,0:T(8,128)(2,1)} %param.29) | copy-start | bytes 1572868
  (66 other events, 624.8 us)
Sparse Core Ops, SparseCore 0:
  10.9 203.7 all-gather.4
  217.8 131.1 all-gather.6
  625.5 61.7 reduce-scatter.15
  691.1 60.1 reduce-scatter.13
  768.3 118.5 all-reduce.21
  889.7 708.8 reduce-scatter.11
  1601.5 1467.7 reduce-scatter.9
where the time goes:
time: 3090 us; the launch traced here: 3080 us
  waiting for transfers between devices  2340 us (76%)
  blocking collectives  320 us (10%)
  matrix products  173 us (6%)
  other arithmetic  98.4 us (3%)
  local copies, waits for them, and re-layouts  75.9 us (2%)
  starting transfers between devices  52 us (2%)
    reduce_scatter x1, waiting for transfers between devices, shards(): lax.psum_scatter(w_in_term, ('dp', 'heads'), scatter_dimension=0, tiled=T...  1470 us
    reduce_scatter x1, waiting for transfers between devices, shards(): lax.psum_scatter(w_out_term, ('dp', 'heads'), scatter_dimension=0, tiled=...  642 us
    unnamed x10, waiting for transfers between devices  118 us
    all_gather x1, waiting for transfers between devices, shards(): lax.all_gather(w_in, ('dp', 'heads'), axis=0, tiled=True)  94 us
    unnamed x2, blocking collectives  90.2 us
    all_gather x1, blocking collectives, shards(): lax.all_gather(gate_w, ('dp', 'heads'), axis=0, tiled=True)  67.5 us
    all_gather x1, blocking collectives, shards(): lax.all_gather(c_low, 'heads', axis=0, tiled=True)  65.8 us
    all_gather x1, blocking collectives, shards(): lax.all_gather(conv_w, ('dp', 'heads'), axis=1, tiled=True)  63.8 us
  transfers between devices with their start and end apart: 15, of which 6 were waited for; matrix products, arithmetic and copies ran while one was open for 7% of the time, Pallas kernels for 0%

commit v1 on v0

v1 whole, which is shorter than its diff:
```python
import numpy as np

import jax
import jax.numpy as jnp
from jax import lax
from jax.sharding import PartitionSpec as P

P_SIZE = 64
N = 128
CONV_K = 4
BLOCK_LEN = 256
SEQS = 3
DI = 4096
CONV_CH = 4352
LANE = 128
EPS = 1e-05

BF = jnp.bfloat16
F32 = jnp.float32


def ring_order(n):
    return list(range(0, n, 2)) + list(range(n - 1, 0, -2))


def ring_place(n):
    order = ring_order(n)
    place = np.zeros(n, np.int32)
    for position, index in enumerate(order):
        place[index] = position
    return np.array(order, np.int32), place


def ring_route(n, step):
    order = ring_order(n)
    return [(order[i], order[(i + step) % n]) for i in range(n)]


def xor_route(n, bits):
    return [(i, i ^ bits) for i in range(n)]


def gather_ring(block, axis, finish):
    n = lax.axis_size(axis)
    order, place = ring_place(n)
    order, mine = jnp.asarray(order), jnp.asarray(place)[lax.axis_index(axis)]
    half = n // 2
    results = [finish(block, lax.axis_index(axis))]
    ahead = behind = block
    for step in range(1, half + 1):
        ahead = lax.ppermute(ahead, axis, ring_route(n, 1))
        results.append(finish(ahead, order[(mine - step) % n]))
        if step < n - half:
            behind = lax.ppermute(behind, axis, ring_route(n, -1))
            results.append(finish(behind, order[(mine + step) % n]))
    return results


def gather_heads(block, axis):
    n = lax.axis_size(axis)
    out = jnp.zeros((n,) + block.shape, block.dtype)
    for part, owner in gather_ring(block, axis, lambda part, owner: (part, owner)):
        out = lax.dynamic_update_slice(out, part[None], (owner, 0, 0))
    return out


def scatter_ring(parts, axis):
    n = lax.axis_size(axis)
    order, place = ring_place(n)
    order, mine = jnp.asarray(order), jnp.asarray(place)[lax.axis_index(axis)]
    half = n // 2

    def shard(position):
        return lax.dynamic_index_in_dim(parts, order[position % n], 0, False)

    ahead, behind = shard(mine + half), shard(mine - (n - half - 1))
    for step in range(1, half + 1):
        ahead = lax.ppermute(ahead, axis, ring_route(n, 1))
        if step < half:
            term = shard(mine + half - step)
            ahead = (ahead.astype(F32) + term.astype(F32)).astype(parts.dtype)
    for step in range(1, n - half):
        behind = lax.ppermute(behind, axis, ring_route(n, -1))
        if step < n - half - 1:
            term = shard(mine - (n - half - 1) + step)
            behind = (behind.astype(F32) + term.astype(F32)).astype(parts.dtype)
    return shard(mine).astype(F32) + ahead.astype(F32) + behind.astype(F32)


def gather_dp(block):
    n = lax.axis_size("dp")
    me = lax.axis_index("dp")
    out = jnp.zeros((n,) + block.shape, block.dtype)
    moving = block
    for step in range(n // 2):
        if step:
            moving = lax.ppermute(moving, "dp", [(i, (i + 2) % n) for i in range(n)])
        other = lax.ppermute(moving, "dp", xor_route(n, 1))
        owner = (me - 2 * step) % n
        out = lax.dynamic_update_slice(out, moving[None], (owner, 0, 0))
        out = lax.dynamic_update_slice(out, other[None], (owner ^ 1, 0, 0))
    return out


def scatter_dp(parts):
    n = lax.axis_size("dp")
    me = lax.axis_index("dp")
    chips = n // 2
    paired = parts.reshape((chips, 2) + parts.shape[1:])
    kept = lax.dynamic_index_in_dim(paired, me % 2, 1, False)
    given = lax.dynamic_index_in_dim(paired, 1 - me % 2, 1, False)
    summed = kept.astype(F32) + lax.ppermute(given, "dp", xor_route(n, 1)).astype(F32)

    def shard(position):
        return lax.dynamic_index_in_dim(summed, position % chips, 0, False)

    chip = me // 2
    moving = shard(chip - 1 + chips)
    for step in range(1, chips):
        arrived = lax.ppermute(moving.astype(parts.dtype), "dp", [(i, (i + 2) % n) for i in range(n)])
        moving = arrived.astype(F32) + shard(chip - 1 - step + 2 * chips)
    return moving


def gather_small(block, axis):
    n = lax.axis_size(axis)
    me = lax.axis_index(axis)
    held = block[None]
    bits = 1
    while bits < n:
        other = lax.ppermute(held, axis, xor_route(n, bits))
        upper = (me & bits) > 0
        held = jnp.where(upper, jnp.concatenate([other, held]), jnp.concatenate([held, other]))
        bits *= 2
    return held


def sum_small(block, axis):
    n = lax.axis_size(axis)
    block = block + lax.ppermute(block, axis, xor_route(n, 1))
    total = block
    for bits in range(2, n, 2):
        total = total + lax.ppermute(block, axis, xor_route(n, bits))
    return total


def packed(arrays):
    flat = jnp.concatenate([a.astype(F32).reshape(-1) for a in arrays])
    flat = jnp.pad(flat, (0, -flat.shape[0] % LANE))
    return flat.reshape(-1, LANE)


def segment_of(positions, seq_ends):
    return jnp.sum((positions[:, None] >= seq_ends[None, :]).astype(jnp.int32), axis=1)


def conv_apply(conv_in, seg, conv_taps, conv_bias):
    rows = conv_in.shape[0]
    extended = jnp.pad(conv_in, ((CONV_K - 1, 0), (0, 0)))
    seg_ext = jnp.pad(seg, (CONV_K - 1, 0), constant_values=-1)
    total = jnp.zeros((rows, conv_in.shape[1]), conv_in.dtype) + conv_bias[None, :]
    for tap_index in range(CONV_K):
        same_seg = (seg_ext[tap_index : tap_index + rows] == seg)[:, None]
        total = total + jnp.where(
            same_seg, conv_taps[tap_index][None, :] * extended[tap_index : tap_index + rows], 0.0
        )
    return jax.nn.silu(total)


def ssd_scan(x_heads, dt_heads, a_neg, b_state, c_state, seg_group, skip_part):
    length, head_count, head_width = x_heads.shape
    blocks = length // BLOCK_LEN
    x_block = x_heads.reshape(blocks, BLOCK_LEN, head_count, head_width)
    dt_block = dt_heads.reshape(blocks, BLOCK_LEN, head_count)
    cum_decay = jnp.cumsum(dt_block * a_neg[None, None, :], axis=1)
    b_block = b_state.reshape(blocks, BLOCK_LEN, b_state.shape[1])
    c_block = c_state.reshape(blocks, BLOCK_LEN, c_state.shape[1])
    seg_block = seg_group.reshape(blocks, BLOCK_LEN)
    positions_in = jnp.arange(BLOCK_LEN, dtype=jnp.int32)
    linked = (seg_block[:, :, None] == seg_block[:, None, :]) & (
        positions_in[:, None] >= positions_in[None, :]
    )[None]
    linked = linked[..., None]
    log_gaps = cum_decay[:, :, None, :] - cum_decay[:, None, :, :]
    decays = jnp.where(linked, jnp.exp(jnp.where(linked, log_gaps, 0.0)), 0.0)
    scores = jnp.einsum("cqn,csn->cqs", c_block, b_block)
    mixing = scores[..., None] * decays * dt_block[:, None, :, :]
    inner_part = jnp.einsum("cqsh,cshp->cqhp", mixing, x_block)
    last_seg = seg_block[:, -1:]
    tail_weight = (
        jnp.where(
            (seg_block == last_seg)[..., None], jnp.exp(cum_decay[:, -1:, :] - cum_decay), 0.0
        )
        * dt_block
    )
    states = jnp.einsum("csn,csh,cshp->chpn", b_block, tail_weight, x_block)
    prev_end = jnp.concatenate([jnp.full((1,), -1, jnp.int32), seg_block[:-1, -1]])
    carry_keep = jnp.where(
        (seg_block[:, -1] == prev_end)[:, None], jnp.exp(cum_decay[:, -1, :]), 0.0
    )

    def advance(carried, inputs):
        block_state, block_keep = inputs
        return (block_state + block_keep[:, None, None] * carried, carried)

    start_state = jnp.zeros(states.shape[1:], states.dtype)
    _, entering = lax.scan(advance, start_state, (states, carry_keep))
    enter_weight = jnp.where((seg_block == prev_end[:, None])[..., None], jnp.exp(cum_decay), 0.0)
    outer_part = jnp.einsum("cqn,chpn->cqhp", c_block, entering) * enter_weight[..., None]
    result = inner_part + outer_part + skip_part[None, None, :, None] * x_block
    return result.reshape(length, head_count, head_width)


def after(value, *others):
    return lax.optimization_barrier((value,) + others)[0]


def shards(
    hidden, seq_lens, norm_w, w_in, conv_w, conv_b, dt_bias, a_log, skip_gain, gate_w, w_out, cotangent
):
    dp, heads = lax.axis_size("dp"), lax.axis_size("heads")
    my_dp, my_head = lax.axis_index("dp"), lax.axis_index("heads")
    me = my_dp * heads + my_head
    rows_dev, width = hidden.shape
    length = rows_dev * heads
    w_rows = w_in.shape[0]
    out_rows = w_out.shape[0]
    own = DI // heads
    own_heads = own // P_SIZE
    taps_dev = conv_b.shape[0]
    striped = out_rows % P_SIZE == 0
    per_block = own_heads // dp if striped else 0

    def split_own(array, size):
        rows = array.shape[0]
        if striped:
            cut = array.reshape(rows, dp, heads, per_block * size).transpose(2, 0, 1, 3)
        else:
            cut = array.reshape(rows, heads, own_heads * size).transpose(1, 0, 2)
        return cut.reshape(heads, rows, own_heads * size)

    def join_own(array, size):
        rows = array.shape[1]
        if striped:
            cut = array.reshape(heads, rows, dp, per_block * size).transpose(1, 2, 0, 3)
        else:
            cut = array.transpose(1, 0, 2)
        return cut.reshape(rows, heads * own_heads * size)

    def pick_own(row, size):
        return lax.dynamic_index_in_dim(split_own(row.reshape(1, -1), size), my_head, 0, False)[0]

    small = packed([conv_w, conv_b, norm_w, gate_w, dt_bias, a_log, skip_gain])
    small_all = gather_small(gather_small(small, "heads").reshape(-1, LANE), "dp")
    small_all = small_all.reshape(dp * heads, -1)
    marks = np.cumsum([0, 4 * taps_dev, taps_dev, w_rows, out_rows] + 3 * [dt_bias.shape[0]])
    pieces = [small_all[:, marks[i] : marks[i + 1]] for i in range(7)]
    taps_full = pieces[0].reshape(-1, CONV_K, taps_dev).transpose(1, 0, 2).reshape(CONV_K, CONV_CH)
    bias_full = pieces[1].reshape(-1)
    norm_full = pieces[2].reshape(-1)
    gate_gain = pick_own(pieces[3], P_SIZE)
    head_params = [pick_own(p[:heads], 1) for p in pieces[4:]]

    def pick_channels(array):
        split = split_own(array[:, :DI], P_SIZE)
        mine = lax.dynamic_index_in_dim(split, my_head, 0, False)
        return jnp.concatenate([mine, array[:, DI:]], axis=1)

    taps_own = pick_channels(taps_full)
    bias_own = pick_channels(bias_full[None])[0]

    pad = LANE - own_heads
    w_gate_cut = split_own(w_in[:, :DI], P_SIZE)
    w_mix_cut = jnp.concatenate(
        [
            split_own(w_in[:, DI : 2 * DI], P_SIZE),
            jnp.broadcast_to(w_in[None, :, 2 * DI : DI + CONV_CH], (heads, w_rows, 2 * N)),
            split_own(w_in[:, DI + CONV_CH :], 1),
            jnp.zeros((heads, w_rows, pad), BF),
        ],
        axis=2,
    )

    def spread(cut):
        got = lax.all_to_all(cut, "heads", split_axis=0, concat_axis=0, tiled=True)
        return gather_dp(got.reshape(heads * w_rows, -1)).reshape(width, -1)

    w_mix = spread(w_mix_cut)
    hidden_all = gather_heads(hidden, "heads").reshape(length, width)
    w_gate = spread(after(w_gate_cut, w_mix))
    if striped:
        w_out_own = gather_dp(w_out).reshape(own, width)
    else:
        route = [(q, (q % dp) * heads + q // dp) for q in range(dp * heads)]
        w_out_own = gather_dp(lax.ppermute(w_out, ("dp", "heads"), route)).reshape(own, width)
    cot_all = gather_heads(after(cotangent, hidden_all), "heads").reshape(length, width)

    seq_ends = jnp.cumsum(seq_lens[0])
    seg = segment_of(jnp.arange(length, dtype=jnp.int32), seq_ends)
    seg_mine = lax.dynamic_slice(seg, (my_head * rows_dev,), (rows_dev,))
    live = (seg < SEQS)[:, None]
    live_mine = (seg_mine < SEQS)[:, None]

    hidden_f = hidden_all.astype(F32)
    scale = lax.rsqrt(jnp.mean(hidden_f * hidden_f, axis=-1, keepdims=True) + EPS)
    normed = (hidden_f * scale * norm_full[None]).astype(BF)
    mix = jnp.dot(normed, w_mix, preferred_element_type=F32)
    conv_in = mix[:, : own + 2 * N]
    dt_low = mix[:, own + 2 * N : own + 2 * N + own_heads].astype(BF)

    def conv_local(rows_in, taps_in, bias_in):
        return conv_apply(rows_in, seg, taps_in, bias_in)

    conv_out, conv_pull = jax.vjp(conv_local, conv_in, taps_own, bias_own)
    conv_low = conv_out.astype(BF).astype(F32)

    def scan_local(conv_rows, dt_in, bias_in, log_in, skip_in):
        mixed = ssd_scan(
            conv_rows[:, :own].reshape(length, own_heads, P_SIZE),
            jax.nn.softplus(dt_in + bias_in[None, :]),
            -jnp.exp(log_in),
            conv_rows[:, own : own + N],
            conv_rows[:, own + N :],
            seg,
            skip_in,
        )
        return mixed.reshape(length, own)

    scanned, scan_pull = jax.vjp(scan_local, conv_low, dt_low.astype(F32), *head_params)
    scanned = scanned.astype(BF).astype(F32)
    gate_part = jnp.dot(normed, w_gate, preferred_element_type=F32)
    gate_sig = jax.nn.sigmoid(gate_part)
    gate_act = gate_part * gate_sig
    inner = scanned * gate_act
    raw = (inner * gate_gain[None]).astype(BF)
    branch = jnp.dot(raw, w_out_own, preferred_element_type=F32).astype(BF)
    branch_mine = scatter_ring(branch.reshape(heads, rows_dev, width), "heads")

    grad_branch = jnp.where(live, cot_all, jnp.zeros_like(cot_all))
    grad_gated = lax.dot_general(
        grad_branch, w_out_own, (((1,), (1,)), ((), ())), preferred_element_type=F32
    )
    weighted = grad_gated * gate_gain[None]
    sums = jnp.stack([jnp.sum(inner * inner, axis=1), jnp.sum(inner * weighted, axis=1)])
    sums = sum_small(sums.reshape(-1, LANE), "heads").reshape(2, length)
    ratio = lax.rsqrt(sums[0] / DI + EPS)
    pull = ratio * ratio * ratio * sums[1] / DI
    ratio_mine = lax.dynamic_slice(ratio, (my_head * rows_dev,), (rows_dev,))[:, None]
    ratio, pull = ratio[:, None], pull[:, None]
    output = (hidden.astype(F32) + jnp.where(live_mine, branch_mine * ratio_mine, 0.0)).astype(BF)
    gated = (inner * ratio * gate_gain[None]).astype(BF)
    contract_first = (((0,), (0,)), ((), ()))
    w_out_term = lax.dot_general(gated, grad_branch, contract_first, preferred_element_type=F32)
    w_out_grad = scatter_dp(w_out_term.astype(BF).reshape(dp, out_rows, width))
    if not striped:
        back = [(dst, src) for src, dst in route]
        w_out_grad = lax.ppermute(w_out_grad, ("dp", "heads"), back)
    gate_w_grad = jnp.sum(w_out.astype(F32) * w_out_grad, axis=1) / gate_w.astype(F32)
    grad_inner = ratio * weighted - inner * pull
    grad_scan = (grad_inner * gate_act).astype(BF)
    grad_gate = (grad_inner * scanned * gate_sig * (1.0 + gate_part * (1.0 - gate_sig))).astype(BF)

    grad_conv, grad_dt, grad_bias, grad_log, grad_skip = scan_pull(grad_scan.astype(F32))
    grad_x = grad_conv[:, :own].astype(BF).astype(F32)
    grad_conv = jnp.concatenate([grad_x, grad_conv[:, own:]], axis=1)
    grad_conv_in, grad_taps, grad_biases = conv_pull(grad_conv)
    grad_mix = jnp.concatenate(
        [grad_conv_in, grad_dt, jnp.zeros((length, pad), F32)], axis=1
    ).astype(BF)

    contract_last = (((1,), (1,)), ((), ()))

    def to_rows(term):
        cols = term.shape[1]
        summed = scatter_dp(term.astype(BF).reshape(dp, heads * w_rows, cols)).astype(BF)
        cut = summed.reshape(heads, w_rows, cols)
        return lax.all_to_all(cut, "heads", split_axis=0, concat_axis=0, tiled=True).astype(F32)

    gate_cols = to_rows(lax.dot_general(normed, grad_gate, contract_first, preferred_element_type=F32))
    grad_normed = lax.dot_general(
        grad_gate, w_gate, contract_last, preferred_element_type=F32
    ) + lax.dot_general(grad_mix, w_mix, contract_last, preferred_element_type=F32)
    grad_mine = scatter_ring(grad_normed.astype(BF).reshape(heads, rows_dev, width), "heads")
    mix_cols = to_rows(lax.dot_general(normed, grad_mix, contract_first, preferred_element_type=F32))
    w_in_grad = jnp.concatenate(
        [
            join_own(gate_cols, P_SIZE),
            join_own(mix_cols[:, :, :own], P_SIZE),
            jnp.sum(mix_cols[:, :, own : own + 2 * N], axis=0),
            join_own(mix_cols[:, :, own + 2 * N : own + 2 * N + own_heads], 1),
        ],
        axis=1,
    )
    norm_w_grad = jnp.sum(w_in.astype(F32) * w_in_grad, axis=1) / norm_w.astype(F32)

    residual = hidden.astype(F32)
    scale_mine = lax.rsqrt(jnp.mean(residual * residual, axis=-1, keepdims=True) + EPS)
    grad_mine = grad_mine * norm_full[None]
    along = jnp.mean(residual * grad_mine, axis=-1, keepdims=True)
    input_grad = cotangent.astype(F32) + scale_mine * (
        grad_mine - residual * (scale_mine * scale_mine * along)
    )

    sent = packed([grad_taps, grad_biases, grad_bias, grad_log, grad_skip])
    summed = sum_small(sent, "dp")
    collected = gather_small(summed, "heads").reshape(heads, -1)
    mine_ch = own + 2 * N
    conv_grads = collected[:, : (CONV_K + 1) * mine_ch].reshape(heads, CONV_K + 1, mine_ch)
    conv_grads = jnp.concatenate(
        [join_own(conv_grads[:, :, :own], P_SIZE), jnp.sum(conv_grads[:, :, own:], axis=0)], axis=1
    )
    conv_grads = lax.dynamic_slice(conv_grads, (0, me * taps_dev), (CONV_K + 1, taps_dev))
    at = (CONV_K + 1) * mine_ch
    head_grads = collected[:, at : at + 3 * own_heads].reshape(heads, 3, own_heads)
    head_grads = join_own(head_grads, 1)
    head_grads = lax.dynamic_slice(head_grads, (0, my_head * own_heads), (3, own_heads))
    return (
        output,
        input_grad,
        norm_w_grad,
        w_in_grad,
        conv_grads[:CONV_K],
        conv_grads[CONV_K],
        head_grads[0],
        head_grads[1],
        head_grads[2],
        gate_w_grad,
        w_out_grad,
    )


def solution(mesh):
    both = ("dp", "heads")
    placed = (
        P(both, None),
        P("dp", None),
        P(both),
        P(both, None),
        P(None, both),
        P(both),
        P("heads"),
        P("heads"),
        P("heads"),
        P(both),
        P(both, None),
        P(both, None),
    )
    return jax.shard_map(
        shards,
        mesh=mesh,
        in_specs=placed,
        out_specs=(
            P(both, None),
            P(both, None),
            P(both),
            P(both, None),
            P(None, both),
            P(both),
            P("heads"),
            P("heads"),
            P("heads"),
            P(both),
            P(both, None),
        ),
        check_vma=False,
    )
```

time: 3090 us -> 570 us (0.18)
  waiting for transfers between devices: 2340 us -> 136 us
  blocking collectives: 320 us -> 0 us
  matrix products: 173 us -> 79.1 us
  local copies, waits for them, and re-layouts: 75.9 us -> 120 us
    reduce_scatter x2 -> x0, waiting for transfers between devices: 2110 us -> none  [the longest x1 1470 us: shards(): lax.psum_scatter(w_in_term, ('dp', 'heads'), scatter_dimension=0, tiled=T...]
    all_gather x4 -> x0, blocking collectives: 223 us -> none  [the longest x1 67.5 us: shards(): lax.all_gather(gate_w, ('dp', 'heads'), axis=0, tiled=True)]
    ppermute x2 -> x57, waiting for transfers between devices: 0.01 us -> 136 us  [the longest x8 39.3 us: gather_ring(): ahead = lax.ppermute(ahead, axis, ring_route(n, 1))]
    unnamed x10 -> x0, waiting for transfers between devices: 118 us -> none
    dot_general x21, matrix products: 173 us -> 79.1 us  [the longest x3 17.3 us: ssd_scan(): inner_part = jnp.einsum('cqsh,cshp->cqhp', mixing, x_block)]
    all_gather x2 -> x0, waiting for transfers between devices: 94 us -> none  [the longest x1 94 us: shards(): lax.all_gather(w_in, ('dp', 'heads'), axis=0, tiled=True)]
    unnamed x2 -> x0, blocking collectives: 90.2 us -> none
    ppermute x2 -> x57, starting transfers between devices: 7.54 us -> 57.2 us  [the longest x8 13.6 us: gather_small(): other = lax.ppermute(held, axis, xor_route(n, bits))]
  transfers between devices with their start and end apart: 15 -> 61, of which waited for: 6 -> 23; matrix products, arithmetic and copies ran while one was open for 7% -> 50% of each run, Pallas kernels for 0% -> 0%
where the time goes in v1:
time: 570 us; the launch traced here: 559 us
  waiting for transfers between devices  136 us (24%)
  local copies, waits for them, and re-layouts  120 us (21%)
  other arithmetic  103 us (18%)
  matrix products  79.1 us (14%)
  starting transfers between devices  79 us (14%)
  between operations  42.5 us (7%)
    ppermute x8, waiting for transfers between devices, gather_ring(): ahead = lax.ppermute(ahead, axis, ring_route(n, 1))  39.3 us
    ppermute x8, waiting for transfers between devices, scatter_ring(): ahead = lax.ppermute(ahead, axis, ring_route(n, 1))  27.4 us
    ppermute x8, waiting for transfers between devices, gather_small(): other = lax.ppermute(held, axis, xor_route(n, bits))  21.6 us
    ppermute x3, waiting for transfers between devices, scatter_dp(): lax.ppermute(moving.astype(parts.dtype), 'dp', [(i, (i + 2) % n) for i in...  18.7 us
    dynamic_update_slice x16, local copies, waits for them, and re-layouts, gather_heads(): out = lax.dynamic_update_slice(out, part[None], (owner, 0, 0))  17.9 us
    dot_general x3, matrix products, ssd_scan(): inner_part = jnp.einsum('cqsh,cshp->cqhp', mixing, x_block)  17.3 us
    ppermute x3, waiting for transfers between devices, gather_dp(): moving = lax.ppermute(moving, 'dp', [(i, (i + 2) % n) for i in range(n)])  14.8 us
    unnamed x223, local copies, waits for them, and re-layouts  13.6 us
  transfers between devices with their start and end apart: 61, of which 23 were waited for; matrix products, arithmetic and copies ran while one was open for 50% of the time, Pallas kernels for 0%

profile of v1, /device:TPU:16, one launch (start us, length us, event | category | flops | bytes accessed | tf_op | source)
XLA Modules:
  0.0 559.3 jit_solution(7828483430847888854)
XLA Ops:
  9.1 6.3 %all-to-all-start = ((bf16[8,64,896]{2,1,0:T(8,128)(2,1)}), bf16[8,64,896]{2,1,0:T(8,128)(2,1)S(1)}, u32[]{:S(2)}, u32[]{:S(2)}) async-start(bf16[8,64,896]{2,1,0:T(8,128)(2,1)} %maximum_maximum_fusion.3), calls=%async_computation | async-start | bytes 1835008 | tf_op jit(solution)/shard_map/all_to_all | solution.py:285
  27.4 5.2 collective-permute-done.1
  109.6 8.2 %collective-permute-done.9 = bf16[128,2048]{1,0:T(8,128)(2,1)} collective-permute-done((bf16[128,2048]{1,0:T(8,128)(2,1)S(1)}, bf16[128,2048]{1,0:T(8,128)(2,1)}, u32[]{:S(2)}, u32[]{:S(2)}) %collective-permute-start.9) | collective-permute-done | bytes 524320 | tf_op jit(solution)/shard_map/ppermute | solution.py:51
  122.7 7.1 %collective-permute-done.11 = bf16[128,2048]{1,0:T(8,128)(2,1)} collective-permute-done((bf16[128,2048]{1,0:T(8,128)(2,1)}, bf16[128,2048]{1,0:T(8,128)(2,1)}, u32[]{:S(2)}, u32[]{:S(2)}) %collective-permute-start.11) | collective-permute-done | bytes 524320 | tf_op jit(solution)/shard_map/ppermute | solution.py:51
  147.0 12.3 %collective-permute-done.30 = bf16[128,2048]{1,0:T(8,128)(2,1)} collective-permute-done((bf16[128,2048]{1,0:T(8,128)(2,1)S(1)}, bf16[128,2048]{1,0:T(8,128)(2,1)}, u32[]{:S(2)}, u32[]{:S(2)}) %collective-permute-start.30) | collective-permute-done | bytes 524320 | tf_op jit(solution)/shard_map/ppermute | solution.py:51
  163.8 4.5 fusion.143
  168.7 4.7 multiply_convert_fusion.1
  185.9 5.6 all-to-all-start.1
  205.2 12.0 %while.36 = (s32[]{:T(128)}, f32[8,64,128]{2,1,0:T(8,128)S(1)}, f32[4,8,64,128]{3,2,1,0:T(8,128)S(1)}, f32[4,8,1,1]{1,3,2,0:T(1,128)}, f32[4,8,64,128]{3,2,1,0:T(8,128)}, /*index=5*/f32[4,8]{1,0:T(4,128)}) while((s32[]{:T(128)}, f32[8,64,128]{2,1,0:T(8,128)S(1)}, f32[4,8,64,128]{3,2,1,0:T(8,128)S(1)}, ...), condition=%wide.region_6.7_spmd.clone.clone, body=%wide.region_5.6_spmd.clone.sunk.clone | while | flops 262147 | bytes 1311944 | solution.py:207
  228.6 4.8 reshape.666
  238.9 7.6 %collective-permute-done.34 = bf16[128,2048]{1,0:T(8,128)(2,1)S(1)} collective-permute-done((bf16[128,2048]{1,0:T(8,128)(2,1)}, bf16[128,2048]{1,0:T(8,128)(2,1)S(1)}, u32[]{:S(2)}, u32[]{:S(2)}) %collective-permute-start.34) | collective-permute-done | bytes 524320 | tf_op jit(solution)/shard_map/ppermute | solution.py:51
  247.4 4.6 bitcast_select_fusion
  255.1 11.5 %collective-permute-done.16 = bf16[512,512]{1,0:T(8,128)(2,1)S(1)} collective-permute-done((bf16[512,512]{1,0:T(8,128)(2,1)}, bf16[512,512]{1,0:T(8,128)(2,1)S(1)}, u32[]{:S(2)}, u32[]{:S(2)}) %collective-permute-start.16) | collective-permute-done | bytes 524320 | tf_op jit(solution)/shard_map/ppermute | solution.py:97
  271.3 7.2 %multiply_reduce_fusion.10 = (f32[1024]{0:T(1024)S(1)}, f32[1024]{0:T(1024)S(1)}, f32[1024,512]{1,0:T(8,128)}, f32[1024,512]{1,0:T(8,128)}) fusion(f32[512]{0:T(512)S(1)} %bitcast.553, f32[1024,512]{1,0:T(8,128)S(1)} %copy-done.8, f32[1024,512]{1,0:T(8,128)S(1)} %fusion.146, bf16[1024,2048]{1,0:T(8,128)(2,1)S(1)} %bitcast.485, bf16[512,2048]{1,0:T(8,128)(2,1)} %bitcast.77), kind=kOutput, calls=%fused_computation.88 | convolution fusion | flops 2152724480 | bytes 14690304 | tf_op jit(solution)/shard_map/dot_general | solution.py:340
  280.0 4.7 convolution_convert_fusion
  311.0 9.1 %fusion.15 = (f32[4,256,8]{1,2,0:T(8,128)}, f32[4,256,8]{1,2,0:T(8,128)}, f32[4,256,8]{1,2,0:T(8,128)}, bf16[4,256,256]{2,1,0:T(8,128)(2,1)}) fusion(f32[4,256,8]{1,2,0:T(8,128)S(1)} %copy.235, f32[4,256,8]{1,2,0:T(8,128)S(1)} %get-tuple-element.295, f32[4,256,256]{2,1,0:T(8,128)} %copy-done.46, pred[4,256,256]{2,1,0:T(8,128)(4,1)} %compare_and_fusion, ...), kind=kOutput, calls=%fused_computation.31 | convolution fusion | flops 299606016 | bytes 4096000 | tf_op jit(solution)/shard_map/transpose(jvp(cqsh,cshp->cqhp))/dot_general | solution.py:188
  320.1 9.9 %while.37 = (s32[]{:T(128)}, f32[8,64,128]{2,1,0:T(8,128)S(1)}, bf16[4,8,64,128]{3,2,1,0:T(8,128)(2,1)}, f32[4,8]{1,0:T(4,128)S(1)}, f32[4,8,64,128]{3,2,1,0:T(8...) while((s32[]{:T(128)}, f32[8,64,128]{2,1,0:T(8,128)S(1)}, ...), condition=%wide.region_13.14_spmd.clone.clone, body=%wide.region_11.13_spmd.clone.sunk.clone | while | flops 393212 | bytes 1442108 | solution.py:207
  353.9 9.9 %reduce-window.31 = f32[4,8,2,128]{3,1,2,0:T(8,128)S(1)} reduce-window(f32[4,8,2,128]{3,1,2,0:T(8,128)S(1)} %add_bitcast_fusion, f32[]{:T(128)} %constant.490.clone.1), window={size=1x1x1x128 pad=0_0x0_0x0_0x0_127}, to_apply=%region_19.20 | reduce-window | flops 1040384 | bytes 65540 | tf_op jit(solution)/shard_map/reduce-window.3
  368.6 5.6 %multiply_reduce_fusion.3 = (f32[768]{0:T(1024)S(1)}, f32[768]{0:T(1024)S(1)}, f32[768]{0:T(1024)S(1)}, f32[768]{0:T(1024)S(1)}, f32[768]{0:T(1024)S(1)}, /*index=5*/f32[1024,768]{1,0:T(8,128)S(1)}) fusion(f32[1024,768]{1,0:T(8,128)S(1)} %copy-done.2, pred[1024]{0:T(1024)(128)(4,1)S(1)} %copy-done.68, pred[1024]{0:T(1024)(128)(4,1)S(1)} %copy-done.70, ...), kind=kLoop, calls=%fused_computation.58 | loop fusion | flops 17297664 | bytes 15747072 | tf_op jit(solution)/shard_map/transpose(jvp())/reduce_sum | solution.py:165
  377.5 6.8 %fusion.82 = f32[1024,2048]{1,0:T(8,128)} fusion(bf16[2048,896]{1,0:T(8,128)(2,1)S(1)} %bitcast.505, bf16[1024,8]{1,0:T(8,128)(2,1)S(1)} %get-tuple-element.289, bf16[1024,768]{1,0:T(8,128)(2,1)S(1)} %fusion.30, bf16[896]{0:T(1024)(128)(2,1)S(1)} %copy-done.81), kind=kOutput, calls=%fused_computation.170 | convolution fusion | flops 3763601408 | bytes 13649664 | tf_op jit(solution)/shard_map/dot_general | solution.py:382
  384.3 9.2 %convolution_convert_fusion.1 = bf16[2048,896]{1,0:T(8,128)(2,1)} fusion(bf16[1024,2048]{1,0:T(8,128)(2,1)} %bitcast.98, f32[2048]{0:T(1024)S(1)} %mul.466, f32[1024]{0:T(1024)S(1)} %copy-done.87, bf16[1024,8]{1,0:T(8,128)(2,1)S(1)} %get-tuple-element.289, bf16[1024,768]{1,0:T(8,128)(2,1)S(1)} %fusion.30, bf16[896]{0:T(1024)(128)(2,1)S(1)} %copy-done.81), kind=kOutput, calls=%fused_computation.48 | convolution fusion | flops 3773825024 | bytes 9467648 | tf_op jit(solution)/shard_map/dot_general | solution.py:384
  393.6 5.0 convolution_convert_fusion.3
  406.7 5.5 convolution_convert_fusion.2
  420.9 9.7 %collective-permute-start.53 = (f32[2,31,128]{2,1,0:T(8,128)S(1)}, f32[2,31,128]{2,1,0:T(8,128)S(1)}, u32[]{:S(2)}, u32[]{:S(2)}) collective-permute-start(f32[2,31,128]{2,1,0:T(8,128)S(1)} %maximum_select_fusion.6), channel_id=1, source_target_pairs={{0,2},{1,3},{2,0},{3,1},{4,6},{5,7},{6,4},{7,5},{8,10},{9,11},{10,... | collective-permute-start | bytes 95240 | tf_op jit(solution)/shard_map/ppermute | solution.py:131
  432.8 5.0 collective-permute-done.54
  445.6 9.7 %collective-permute-done.22 = bf16[128,2048]{1,0:T(8,128)(2,1)S(1)} collective-permute-done((bf16[128,2048]{1,0:T(8,128)(2,1)S(1)}, bf16[128,2048]{1,0:T(8,128)(2,1)S(1)}, u32[]{:S(2)}, u32[]{:S(2)}) %collective-permute-start.22) | collective-permute-done | bytes 524320 | tf_op jit(solution)/shard_map/ppermute | solution.py:78
  460.2 6.3 %collective-permute-done.40 = bf16[128,2048]{1,0:T(8,128)(2,1)S(1)} collective-permute-done((bf16[128,2048]{1,0:T(8,128)(2,1)S(1)}, bf16[128,2048]{1,0:T(8,128)(2,1)S(1)}, u32[]{:S(2)}, u32[]{:S(2)}) %collective-permute-start.40) | collective-permute-done | bytes 524320 | tf_op jit(solution)/shard_map/ppermute | solution.py:78
  476.6 8.3 %collective-permute-done.47 = bf16[512,512]{1,0:T(8,128)(2,1)S(1)} collective-permute-done((bf16[512,512]{1,0:T(8,128)(2,1)S(1)}, bf16[512,512]{1,0:T(8,128)(2,1)S(1)}, u32[]{:S(2)}, u32[]{:S(2)}) %collective-permute-start.47) | collective-permute-done | bytes 524320 | tf_op jit(solution)/shard_map/ppermute | solution.py:120
  487.3 5.7 %all-to-all-start.2 = ((bf16[8,64,512]{2,1,0:T(8,128)(2,1)}), bf16[8,64,512]{2,1,0:T(8,128)(2,1)S(1)}, u32[]{:S(2)}, u32[]{:S(2)}) async-start(bf16[8,64,512]{2,1,0:T(8,128)(2,1)} %bitcast.147), calls=%async_computation.2 | async-start | bytes 1048576 | tf_op jit(solution)/shard_map/all_to_all | solution.py:377
  497.8 10.4 %collective-permute-done.49 = bf16[512,896]{1,0:T(8,128)(2,1)} collective-permute-done((bf16[512,896]{1,0:T(8,128)(2,1)S(1)}, bf16[512,896]{1,0:T(8,128)(2,1)}, u32[]{:S(2)}, u32[]{:S(2)}) %collective-permute-start.49) | collective-permute-done | bytes 917536 | tf_op jit(solution)/shard_map/ppermute | solution.py:120
  523.3 7.3 %collective-permute-done.42 = bf16[128,2048]{1,0:T(8,128)(2,1)} collective-permute-done((bf16[128,2048]{1,0:T(8,128)(2,1)}, bf16[128,2048]{1,0:T(8,128)(2,1)}, u32[]{:S(2)}, u32[]{:S(2)}) %collective-permute-start.42) | collective-permute-done | bytes 524320 | tf_op jit(solution)/shard_map/ppermute | solution.py:78
  532.4 11.9 %collective-permute-done.27 = bf16[128,2048]{1,0:T(8,128)(2,1)S(1)} collective-permute-done((bf16[128,2048]{1,0:T(8,128)(2,1)S(1)}, bf16[128,2048]{1,0:T(8,128)(2,1)S(1)}, u32[]{:S(2)}, u32[]{:S(2)}) %collective-permute-start.27) | collective-permute-done | bytes 524320 | tf_op jit(solution)/shard_map/ppermute | solution.py:83
  (599 shorter events, 297.1 us)
Async XLA Ops:
  0.7 90.6 %collective-permute-start.5 = (bf16[128,2048]{1,0:T(8,128)(2,1)}, bf16[128,2048]{1,0:T(8,128)(2,1)}, u32[]{:S(2)}, u32[]{:S(2)}) collective-permute-start(bf16[128,2048]{1,0:T(8,128)(2,1)} %param.24), channel_id=1, source_target_pairs={{0,2},{2,4},{4,6},{6,7},{7,5},{5,3},{3,1},{1,0},{8,10},{10,12},{12... | collective-permute-start | bytes 1572872 | tf_op jit(solution)/shard_map/ppermute | solution.py:51
  2.3 90.2 %collective-permute-start.6 = (bf16[128,2048]{1,0:T(8,128)(2,1)}, bf16[128,2048]{1,0:T(8,128)(2,1)}, u32[]{:S(2)}, u32[]{:S(2)}) collective-permute-start(bf16[128,2048]{1,0:T(8,128)(2,1)} %param.24), channel_id=1, source_target_pairs={{0,1},{2,0},{4,2},{6,4},{7,6},{5,7},{3,5},{1,3},{8,9},{10,8},{12,1... | collective-permute-start | bytes 1572872 | tf_op jit(solution)/shard_map/ppermute | solution.py:54
  2.7 94.3 %collective-permute-start.18 = (bf16[128,2048]{1,0:T(8,128)(2,1)}, bf16[128,2048]{1,0:T(8,128)(2,1)}, u32[]{:S(2)}, u32[]{:S(2)}) collective-permute-start(bf16[128,2048]{1,0:T(8,128)(2,1)} %param.34), channel_id=1, source_target_pairs={{0,8},{8,0},{16,24},{24,16},{1,9},{9,1},{17,25},{25,17},{2,10},{10... | collective-permute-start | bytes 1572872 | tf_op jit(solution)/shard_map/ppermute | solution.py:98
  2.7 90.5 %collective-permute-start.19 = (bf16[128,2048]{1,0:T(8,128)(2,1)}, bf16[128,2048]{1,0:T(8,128)(2,1)}, u32[]{:S(2)}, u32[]{:S(2)}) collective-permute-start(bf16[128,2048]{1,0:T(8,128)(2,1)} %param.34), channel_id=1, source_target_pairs={{0,16},{8,24},{16,0},{24,8},{1,17},{9,25},{17,1},{25,9},{2,18},{10... | collective-permute-start | bytes 1572872 | tf_op jit(solution)/shard_map/ppermute | solution.py:97
  9.1 112.6 %all-to-all-start = ((bf16[8,64,896]{2,1,0:T(8,128)(2,1)}), bf16[8,64,896]{2,1,0:T(8,128)(2,1)S(1)}, u32[]{:S(2)}, u32[]{:S(2)}) async-start(bf16[8,64,896]{2,1,0:T(8,128)(2,1)} %maximum_maximum_fusion.3), calls=%async_computation | async-start | bytes 1835008 | tf_op jit(solution)/shard_map/all_to_all | solution.py:285
  37.3 45.8 %collective-permute-start.3 = (f32[1,56,128]{2,1,0:T(8,128)S(1)}, f32[1,56,128]{2,1,0:T(8,128)S(1)}, u32[]{:S(2)}, u32[]{:S(2)}) collective-permute-start(f32[1,56,128]{2,1,0:T(8,128)S(1)} %select_n.610), channel_id=1, source_target_pairs={{0,8},{8,0},{16,24},{24,16},{1,9},{9,1},{17,25},{25,17},{2,10},{10... | collective-permute-start | bytes 86024 | tf_op jit(solution)/shard_map/ppermute | solution.py:131
  121.7 22.8 %collective-permute-start.12 = (bf16[512,896]{1,0:T(8,128)(2,1)S(1)}, bf16[512,896]{1,0:T(8,128)(2,1)S(1)}, u32[]{:S(2)}, u32[]{:S(2)}) collective-permute-start(bf16[512,896]{1,0:T(8,128)(2,1)S(1)} %bitcast.501), channel_id=1, source_target_pairs={{0,8},{8,0},{16,24},{24,16},{1,9},{9,1},{17,25},{25,17},{2,10},{10... | collective-permute-start | bytes 2752520 | tf_op jit(solution)/shard_map/ppermute | solution.py:98
  121.7 22.8 %collective-permute-start.13 = (bf16[512,896]{1,0:T(8,128)(2,1)S(1)}, bf16[512,896]{1,0:T(8,128)(2,1)S(1)}, u32[]{:S(2)}, u32[]{:S(2)}) collective-permute-start(bf16[512,896]{1,0:T(8,128)(2,1)S(1)} %bitcast.502), channel_id=1, source_target_pairs={{0,16},{8,24},{16,0},{24,8},{1,17},{9,25},{17,1},{25,9},{2,18},{10... | collective-permute-start | bytes 2752520 | tf_op jit(solution)/shard_map/ppermute | solution.py:97
  144.5 19.2 %collective-permute-start.14 = (bf16[512,896]{1,0:T(8,128)(2,1)S(1)}, bf16[512,896]{1,0:T(8,128)(2,1)S(1)}, u32[]{:S(2)}, u32[]{:S(2)}) collective-permute-start(bf16[512,896]{1,0:T(8,128)(2,1)S(1)} %collective-permute-done.13), channel_id=1, source_target_pairs={{0,8},{8,0},{16,24},{24,16},{1,9},{9,1},{17,25},{25,17},{2,10},{10... | collective-permute-start | bytes 2752520 | tf_op jit(solution)/shard_map/ppermute | solution.py:98
  159.3 74.1 %collective-permute-start.32 = (bf16[128,2048]{1,0:T(8,128)(2,1)}, bf16[128,2048]{1,0:T(8,128)(2,1)}, u32[]{:S(2)}, u32[]{:S(2)}) collective-permute-start(bf16[128,2048]{1,0:T(8,128)(2,1)} %collective-permute-done.30), channel_id=1, source_target_pairs={{0,2},{2,4},{4,6},{6,7},{7,5},{5,3},{3,1},{1,0},{8,10},{10,12},{12... | collective-permute-start | bytes 1572872 | tf_op jit(solution)/shard_map/ppermute | solution.py:51
  160.7 76.3 %collective-permute-start.33 = (bf16[128,2048]{1,0:T(8,128)(2,1)}, bf16[128,2048]{1,0:T(8,128)(2,1)}, u32[]{:S(2)}, u32[]{:S(2)}) collective-permute-start(bf16[128,2048]{1,0:T(8,128)(2,1)} %collective-permute-done.31), channel_id=1, source_target_pairs={{0,1},{2,0},{4,2},{6,4},{7,6},{5,7},{3,5},{1,3},{8,9},{10,8},{12,1... | collective-permute-start | bytes 1572872 | tf_op jit(solution)/shard_map/ppermute | solution.py:54
  185.9 66.1 %all-to-all-start.1 = ((bf16[8,64,512]{2,1,0:T(8,128)(2,1)}), bf16[8,64,512]{2,1,0:T(8,128)(2,1)}, u32[]{:S(2)}, u32[]{:S(2)}) async-start(bf16[8,64,512]{2,1,0:T(8,128)(2,1)} %reshape.596), calls=%async_computation.1 | async-start | bytes 1048576 | tf_op jit(solution)/shard_map/all_to_all | solution.py:285
  289.8 149.3 %collective-permute-start.21 = (bf16[128,2048]{1,0:T(8,128)(2,1)}, bf16[128,2048]{1,0:T(8,128)(2,1)}, u32[]{:S(2)}, u32[]{:S(2)}) collective-permute-start(bf16[128,2048]{1,0:T(8,128)(2,1)} %get-tuple-element.311), channel_id=1, source_target_pairs={{0,2},{2,4},{4,6},{6,7},{7,5},{5,3},{3,1},{1,0},{8,10},{10,12},{12... | collective-permute-start | bytes 1572872 | tf_op jit(solution)/shard_map/ppermute | solution.py:78
  291.8 153.6 %collective-permute-start.25 = (bf16[128,2048]{1,0:T(8,128)(2,1)}, bf16[128,2048]{1,0:T(8,128)(2,1)}, u32[]{:S(2)}, u32[]{:S(2)}) collective-permute-start(bf16[128,2048]{1,0:T(8,128)(2,1)} %get-tuple-element.312), channel_id=1, source_target_pairs={{0,1},{2,0},{4,2},{6,4},{7,6},{5,7},{3,5},{1,3},{8,9},{10,8},{12,1... | collective-permute-start | bytes 1572872 | tf_op jit(solution)/shard_map/ppermute | solution.py:83
  404.3 38.4 %collective-permute-start.39 = (bf16[128,2048]{1,0:T(8,128)(2,1)}, bf16[128,2048]{1,0:T(8,128)(2,1)}, u32[]{:S(2)}, u32[]{:S(2)}) collective-permute-start(bf16[128,2048]{1,0:T(8,128)(2,1)} %get-tuple-element.305), channel_id=1, source_target_pairs={{0,2},{2,4},{4,6},{6,7},{7,5},{5,3},{3,1},{1,0},{8,10},{10,12},{12... | collective-permute-start | bytes 1572872 | tf_op jit(solution)/shard_map/ppermute | solution.py:78
  415.4 42.6 %collective-permute-start.43 = (bf16[128,2048]{1,0:T(8,128)(2,1)}, bf16[128,2048]{1,0:T(8,128)(2,1)}, u32[]{:S(2)}, u32[]{:S(2)}) collective-permute-start(bf16[128,2048]{1,0:T(8,128)(2,1)} %get-tuple-element.306), channel_id=1, source_target_pairs={{0,1},{2,0},{4,2},{6,4},{7,6},{5,7},{3,5},{1,3},{8,9},{10,8},{12,1... | collective-permute-start | bytes 1572872 | tf_op jit(solution)/shard_map/ppermute | solution.py:83
  437.9 32.0 %collective-permute-start.46 = (bf16[2,512,512]{2,1,0:T(8,128)(2,1)}, bf16[2,512,512]{2,1,0:T(8,128)(2,1)S(1)}, u32[]{:S(2)}, u32[]{:S(2)}) collective-permute-start(bf16[2,512,512]{2,1,0:T(8,128)(2,1)} %dynamic-slice_bitcast_fusion.2), channel_id=1, source_target_pairs={{0,8},{8,0},{16,24},{24,16},{1,9},{9,1},{17,25},{25,17},{2,10},{10... | collective-permute-start | bytes 3145736 | tf_op jit(solution)/shard_map/ppermute | solution.py:112
  444.1 22.5 %collective-permute-start.40 = (bf16[128,2048]{1,0:T(8,128)(2,1)S(1)}, bf16[128,2048]{1,0:T(8,128)(2,1)S(1)}, u32[]{:S(2)}, u32[]{:S(2)}) collective-permute-start(bf16[128,2048]{1,0:T(8,128)(2,1)S(1)} %fusion.63), channel_id=1, source_target_pairs={{0,2},{2,4},{4,6},{6,7},{7,5},{5,3},{3,1},{1,0},{8,10},{10,12},{12... | collective-permute-start | bytes 1572872 | tf_op jit(solution)/shard_map/ppermute | solution.py:78
  445.4 28.4 %collective-permute-start.48 = (bf16[2,512,896]{2,1,0:T(8,128)(2,1)S(1)}, bf16[2,512,896]{2,1,0:T(8,128)(2,1)S(1)}, u32[]{:S(2)}, u32[]{:S(2)}) collective-permute-start(bf16[2,512,896]{2,1,0:T(8,128)(2,1)S(1)} %copy-done.43), channel_id=1, source_target_pairs={{0,8},{8,0},{16,24},{24,16},{1,9},{9,1},{17,25},{25,17},{2,10},{10... | collective-permute-start | bytes 5505032 | tf_op jit(solution)/shard_map/ppermute | solution.py:112
  455.3 16.5 %collective-permute-start.55 = (bf16[2,128,2048]{2,1,0:T(8,128)(2,1)S(1)}, bf16[2,128,2048]{2,1,0:T(8,128)(2,1)S(1)}, u32[]{:S(2)}, u32[]{:S(2)}) collective-permute-start(bf16[2,128,2048]{2,1,0:T(8,128)(2,1)S(1)} %copy-done.45), channel_id=1, source_target_pairs={{0,8},{8,0},{16,24},{24,16},{1,9},{9,1},{17,25},{25,17},{2,10},{10... | collective-permute-start | bytes 3145736 | tf_op jit(solution)/shard_map/ppermute | solution.py:112
  458.0 58.4 %collective-permute-start.23 = (bf16[128,2048]{1,0:T(8,128)(2,1)}, bf16[128,2048]{1,0:T(8,128)(2,1)}, u32[]{:S(2)}, u32[]{:S(2)}) collective-permute-start(bf16[128,2048]{1,0:T(8,128)(2,1)} %get-tuple-element.309), channel_id=1, source_target_pairs={{0,2},{2,4},{4,6},{6,7},{7,5},{5,3},{3,1},{1,0},{8,10},{10,12},{12... | collective-permute-start | bytes 1572872 | tf_op jit(solution)/shard_map/ppermute | solution.py:78
  466.5 50.0 %collective-permute-start.26 = (bf16[128,2048]{1,0:T(8,128)(2,1)}, bf16[128,2048]{1,0:T(8,128)(2,1)}, u32[]{:S(2)}, u32[]{:S(2)}) collective-permute-start(bf16[128,2048]{1,0:T(8,128)(2,1)} %get-tuple-element.310), channel_id=1, source_target_pairs={{0,1},{2,0},{4,2},{6,4},{7,6},{5,7},{3,5},{1,3},{8,9},{10,8},{12,1... | collective-permute-start | bytes 1572872 | tf_op jit(solution)/shard_map/ppermute | solution.py:83
  469.8 24.0 %collective-permute-start.41 = (bf16[128,2048]{1,0:T(8,128)(2,1)}, bf16[128,2048]{1,0:T(8,128)(2,1)}, u32[]{:S(2)}, u32[]{:S(2)}) collective-permute-start(bf16[128,2048]{1,0:T(8,128)(2,1)} %get-tuple-element.303), channel_id=1, source_target_pairs={{0,2},{2,4},{4,6},{6,7},{7,5},{5,3},{3,1},{1,0},{8,10},{10,12},{12... | collective-permute-start | bytes 1572872 | tf_op jit(solution)/shard_map/ppermute | solution.py:78
  473.8 20.6 %collective-permute-start.44 = (bf16[128,2048]{1,0:T(8,128)(2,1)}, bf16[128,2048]{1,0:T(8,128)(2,1)}, u32[]{:S(2)}, u32[]{:S(2)}) collective-permute-start(bf16[128,2048]{1,0:T(8,128)(2,1)} %get-tuple-element.304), channel_id=1, source_target_pairs={{0,1},{2,0},{4,2},{6,4},{7,6},{5,7},{3,5},{1,3},{8,9},{10,8},{12,1... | collective-permute-start | bytes 1572872 | tf_op jit(solution)/shard_map/ppermute | solution.py:83
  484.8 23.4 %collective-permute-start.49 = (bf16[512,896]{1,0:T(8,128)(2,1)S(1)}, bf16[512,896]{1,0:T(8,128)(2,1)}, u32[]{:S(2)}, u32[]{:S(2)}) collective-permute-start(bf16[512,896]{1,0:T(8,128)(2,1)S(1)} %fusion.86), channel_id=1, source_target_pairs={{0,16},{8,24},{16,0},{24,8},{1,17},{9,25},{17,1},{25,9},{2,18},{10... | collective-permute-start | bytes 2752520 | tf_op jit(solution)/shard_map/ppermute | solution.py:120
  487.3 25.0 %all-to-all-start.2 = ((bf16[8,64,512]{2,1,0:T(8,128)(2,1)}), bf16[8,64,512]{2,1,0:T(8,128)(2,1)S(1)}, u32[]{:S(2)}, u32[]{:S(2)}) async-start(bf16[8,64,512]{2,1,0:T(8,128)(2,1)} %bitcast.147), calls=%async_computation.2 | async-start | bytes 1048576 | tf_op jit(solution)/shard_map/all_to_all | solution.py:377
  493.8 26.8 %collective-permute-start.56 = (bf16[128,2048]{1,0:T(8,128)(2,1)}, bf16[128,2048]{1,0:T(8,128)(2,1)}, u32[]{:S(2)}, u32[]{:S(2)}) collective-permute-start(bf16[128,2048]{1,0:T(8,128)(2,1)} %fusion.94), channel_id=1, source_target_pairs={{0,16},{8,24},{16,0},{24,8},{1,17},{9,25},{17,1},{25,9},{2,18},{10... | collective-permute-start | bytes 1572872 | tf_op jit(solution)/shard_map/ppermute | solution.py:120
  497.2 26.1 %collective-permute-start.45 = (bf16[128,2048]{1,0:T(8,128)(2,1)}, bf16[128,2048]{1,0:T(8,128)(2,1)}, u32[]{:S(2)}, u32[]{:S(2)}) collective-permute-start(bf16[128,2048]{1,0:T(8,128)(2,1)} %get-tuple-element.302), channel_id=1, source_target_pairs={{0,1},{2,0},{4,2},{6,4},{7,6},{5,7},{3,5},{1,3},{8,9},{10,8},{12,1... | collective-permute-start | bytes 1572872 | tf_op jit(solution)/shard_map/ppermute | solution.py:83
  508.2 22.4 %collective-permute-start.42 = (bf16[128,2048]{1,0:T(8,128)(2,1)}, bf16[128,2048]{1,0:T(8,128)(2,1)}, u32[]{:S(2)}, u32[]{:S(2)}) collective-permute-start(bf16[128,2048]{1,0:T(8,128)(2,1)} %get-tuple-element.301), channel_id=1, source_target_pairs={{0,2},{2,4},{4,6},{6,7},{7,5},{5,3},{3,1},{1,0},{8,10},{10,12},{12... | collective-permute-start | bytes 1572872 | tf_op jit(solution)/shard_map/ppermute | solution.py:78
  512.3 42.1 %all-to-all-start.3 = ((bf16[8,64,896]{2,1,0:T(8,128)(2,1)}), bf16[8,64,896]{2,1,0:T(8,128)(2,1)S(1)}, u32[]{:S(2)}, u32[]{:S(2)}) async-start(bf16[8,64,896]{2,1,0:T(8,128)(2,1)} %bitcast.506), calls=%async_computation.3 | async-start | bytes 1835008 | tf_op jit(solution)/shard_map/all_to_all | solution.py:377
  518.5 25.8 %collective-permute-start.27 = (bf16[128,2048]{1,0:T(8,128)(2,1)S(1)}, bf16[128,2048]{1,0:T(8,128)(2,1)S(1)}, u32[]{:S(2)}, u32[]{:S(2)}) collective-permute-start(bf16[128,2048]{1,0:T(8,128)(2,1)S(1)} %get-tuple-element.308), channel_id=1, source_target_pairs={{0,1},{2,0},{4,2},{6,4},{7,6},{5,7},{3,5},{1,3},{8,9},{10,8},{12,1... | collective-permute-start | bytes 1572872 | tf_op jit(solution)/shard_map/ppermute | solution.py:83
  519.1 29.4 %collective-permute-start.24 = (bf16[128,2048]{1,0:T(8,128)(2,1)S(1)}, bf16[128,2048]{1,0:T(8,128)(2,1)S(1)}, u32[]{:S(2)}, u32[]{:S(2)}) collective-permute-start(bf16[128,2048]{1,0:T(8,128)(2,1)S(1)} %get-tuple-element.307), channel_id=1, source_target_pairs={{0,2},{2,4},{4,6},{6,7},{7,5},{5,3},{3,1},{1,0},{8,10},{10,12},{12... | collective-permute-start | bytes 1572872 | tf_op jit(solution)/shard_map/ppermute | solution.py:78
  (134 other events, 1896.4 us)
